TPU v7x, 32 devices: a whole 2x2x4 slice. The times are simulated.
32 devices in a mesh: pop: 2 (over x), blk: 16 (over z, y, core).
Axes of the slice: x: 2, y: 2, z: 4, core: 2. Of those that a mesh axis runs over, the one named last changes fastest.
Arguments:
- v_init: float32 [128, 2, 16384], P('pop', None, 'blk'), may hold values from -6 to 6
- a_init: float32 [128, 2, 16384], P('pop', None, 'blk'), may hold values from 0 to 1
- z_init: bfloat16 [128, 2, 16384], P('pop', None, 'blk'), may hold values from 0 to 1
- base_weight: bfloat16 [16384, 16384], P('blk', 'pop'), may hold values from -0.046875 to 0.046875
- factor_u: bfloat16 [128, 4, 16384], P('pop', None, 'blk'), may hold values from -6 to 6
- factor_v: bfloat16 [128, 4, 16384], P('pop', None, 'blk'), may hold values from -0.046875 to 0.046875
- in_weight: bfloat16 [700, 16384], P(None, 'blk'), may hold values from -0.21875 to 0.21875
- spikes_in: int32 [2, 2, 700], replicated, may hold values 0 or 1
- step_count: int32 [128, 2], P('pop'), may hold values from 1 to 2, as said below
- member_ids: int32 [128], P('pop'), may hold values from 0 to 127, each once
- decay_mem: float32 [16384], P('blk'), may hold values from 0.3 to 0.9
- decay_adapt: float32 [16384], P('blk'), may hold values from 0.5 to 0.95
- thr_base: float32 [16384], P('blk'), may hold values from 0.2 to 1
- thr_adapt: float32 [16384], P('blk'), may hold values from 0.5 to 2
Outputs:
- v_out: float32 [128, 2, 16384], P('pop', None, 'blk')
- a_out: float32 [128, 2, 16384], P('pop', None, 'blk')
Inputs may be any that keep to these rules, and one draw needn't show every extreme that they name: `member_ids`: each member appears in exactly one slot. `step_count`: a trial's state stops changing after its last step.
All inputs are finite; a program needn't handle non-finite values.
Results may differ from a plain program's by a relative error of at most 0.00088.
Values may be sent and summed in bfloat16 or wider, within the bound.
A program may use at most 128 MiB of HBM per device.

v0:
```python
import jax
import jax.numpy as jnp
from jax import lax
from jax.sharding import PartitionSpec as P

STEPS = 2


def body(
    v_init,
    a_init,
    z_init,
    base_weight,
    factor_u,
    factor_v,
    in_weight,
    spikes_in,
    step_count,
    member_ids,
    decay_mem,
    decay_adapt,
    thr_base,
    thr_adapt,
):
    members, trials, block = v_init.shape
    rows = members * trials
    sign = (1 - 2 * (member_ids % 2)).astype(jnp.float32)
    panel = lax.all_gather(base_weight, "pop", axis=1, tiled=True)
    state_v, state_a, spikes = (v_init, a_init, z_init)
    for step in range(STEPS):
        spikes_f = spikes.astype(jnp.float32)
        partial_value = jnp.einsum(
            "mtn,mkn->mtk", spikes, factor_v, preferred_element_type=jnp.float32
        )
        proj = lax.psum(partial_value, "blk").astype(jnp.bfloat16)
        low = jnp.einsum("mtk,mkn->mtn", proj, factor_u, preferred_element_type=jnp.float32)
        spike_rows = spikes.reshape(rows, block)
        total = lax.dot_general(
            lax.all_gather(spike_rows, "blk", axis=1, tiled=True),
            panel,
            (((1,), (1,)), ((), ())),
            preferred_element_type=jnp.float32,
        )
        dense = total.reshape(members, trials, block)
        current = jnp.dot(
            spikes_in[step].astype(jnp.bfloat16), in_weight, preferred_element_type=jnp.float32
        )
        drive = dense + 0.5 * sign[:, None, None] * low + current[None]
        v_new = (
            decay_mem * state_v
            + (1.0 - decay_mem) * drive
            - spikes_f * (thr_base + thr_adapt * state_a)
        )
        a_new = decay_adapt * state_a + (1.0 - decay_adapt) * spikes_f
        active = (step_count > step)[:, :, None]
        state_v = jnp.where(active, v_new, state_v)
        state_a = jnp.where(active, a_new, state_a)
        if step + 1 < STEPS:
            spikes = jax.nn.sigmoid(3.0 * (state_v - thr_base - thr_adapt * state_a)).astype(
                jnp.bfloat16
            )
    return (state_v, state_a)


def solution(mesh):
    in_specs = (
        P("pop", None, "blk"),
        P("pop", None, "blk"),
        P("pop", None, "blk"),
        P("blk", "pop"),
        P("pop", None, "blk"),
        P("pop", None, "blk"),
        P(None, "blk"),
        P(),
        P("pop", None),
        P("pop"),
        P("blk"),
        P("blk"),
        P("blk"),
        P("blk"),
    )
    out_specs = (P("pop", None, "blk"), P("pop", None, "blk"))
    return jax.shard_map(body, mesh=mesh, in_specs=in_specs, out_specs=out_specs, check_vma=False)
```

profile of v0, /device:TPU:0, one launch (start us, length us, event | category | flops | bytes accessed | tf_op | source)
XLA Modules:
  0.0 567.9 jit_solution(5290168051296004160)
XLA Ops:
  7.2 0.0 copy-start
  7.2 0.0 all-gather.4.cloned.1.call-start
  7.2 1.9 reshape.30
  9.1 0.0 all-gather.4.cloned.1.call-update
  9.1 0.0 copy-start.5
  9.1 0.0 copy-start.2
  9.1 0.0 copy-start.1
  9.1 0.0 copy-start.6
  9.2 0.0 copy-start.9
  9.2 0.0 copy-start.3
  9.2 0.0 copy-start.4
  9.2 0.0 all-gather.6.cloned.1.call-start
  9.2 0.7 all-gather.6.cloned.1.call-update
  9.9 0.0 all-gather.8.cloned.1.call-start
  10.0 0.0 copy-done.5
  10.0 0.1 copy.16
  10.1 0.1 copy.17
  10.2 0.0 copy-done.2
  10.3 0.0 copy-done.1
  10.3 0.0 copy-done.6
  10.3 0.6 fusion.28
  10.9 63.7 %psum.14 = bf16[64,2,4]{2,1,0:T(2,128)(2,1)S(1)} all-reduce(f32[64,2,4]{2,1,0:T(2,128)S(1)} %fusion.28), channel_id=1, replica_groups=mesh['pop'=2,'blk'=16] {'blk'}, use_global_device_ids=true, to_apply=%region_0.1 | all-reduce | flops 512 | bytes 3072 | tf_op jit(solution)/shard_map/psum | solution.py:35
  74.6 0.0 copy-done.9
  74.6 0.0 copy-done.3
  74.6 0.0 copy-done.4
  74.7 0.0 copy-done
  74.7 0.3 fusion.20
  75.0 0.0 copy-start.7
  75.0 0.0 copy-start.8
  75.0 0.0 all-gather.4.cloned.1.call-done
  75.0 378.5 %all-gather.6.cloned.1.call-done = bf16[1024,16384]{1,0:T(8,128)(2,1)} async-done(((bf16[1024,8192]{1,0:T(8,128)(2,1)}), bf16[1024,16384]{1,0:T(8,128)(2,1)}) %all-gather.6.cloned.1.call-update) | async-done | bytes 33554448 | tf_op jit(solution)/shard_map/all_gather | solution.py:28
  453.5 16.9 %fusion.27 = f32[128,1024]{1,0:T(8,128)S(1)} fusion(bf16[128,16384]{1,0:T(8,128)(2,1)} %all-gather.4.cloned.1.call-done, bf16[1024,16384]{1,0:T(8,128)(2,1)} %all-gather.6.cloned.1.call-done), kind=kOutput, calls=%fused_computation.42 | convolution fusion | flops 4294967296 | bytes 38273024 | tf_op jit(solution)/shard_map/dot_general | solution.py:38
  470.4 0.3 reshape.31
  470.7 0.0 copy-done.7
  470.7 0.0 copy-done.8
  470.8 4.6 fusion.15
  475.4 0.8 reshape.32
  476.2 0.0 all-gather.8.cloned.1.call-update
  476.2 0.3 fusion.19
  476.5 1.7 fusion.30
  478.2 62.1 %psum.15 = bf16[64,2,4]{2,1,0:T(2,128)(2,1)S(1)} all-reduce(f32[64,2,4]{2,1,0:T(2,128)S(1)} %fusion.30), channel_id=1, replica_groups=mesh['pop'=2,'blk'=16] {'blk'}, use_global_device_ids=true, to_apply=%region_1.2 | all-reduce | flops 512 | bytes 3072 | tf_op jit(solution)/shard_map/psum | solution.py:35
  540.3 0.0 all-gather.8.cloned.1.call-done
  540.3 16.9 %fusion.29 = f32[128,1024]{1,0:T(8,128)S(1)} fusion(bf16[128,16384]{1,0:T(8,128)(2,1)} %all-gather.8.cloned.1.call-done, bf16[1024,16384]{1,0:T(8,128)(2,1)} %all-gather.6.cloned.1.call-done), kind=kOutput, calls=%fused_computation.44 | convolution fusion | flops 4294967296 | bytes 38273024 | tf_op jit(solution)/shard_map/dot_general | solution.py:38
  557.2 0.3 reshape.33
  557.5 3.8 fusion.11
  (5 shorter events, 0.0 us)
Async XLA Ops:
  7.2 67.5 %copy-start = (bf16[700,1024]{1,0:T(8,128)(2,1)S(1)}, bf16[700,1024]{1,0:T(8,128)(2,1)}, u32[]{:S(2)}) copy-start(bf16[700,1024]{1,0:T(8,128)(2,1)} %param.20) | copy-start | bytes 4300804
  7.2 67.8 %all-gather.4.cloned.1.call-start = ((), (), s32[]{:S(2)}) async-start(), calls=%async_computation | async-start | bytes 4456448 | tf_op jit(solution)/shard_map/all_gather | solution.py:39
  9.1 0.9 copy-start.5
  9.1 1.1 copy-start.2
  9.1 1.1 copy-start.1
  9.1 1.1 copy-start.6
  9.2 65.5 %copy-start.9 = (s32[64]{0:T(128)S(1)}, s32[64]{0:T(128)}, u32[]{:S(2)}) copy-start(s32[64]{0:T(128)} %param.23) | copy-start | bytes 772
  9.2 65.5 %copy-start.3 = (f32[1024]{0:T(1024)S(1)}, f32[1024]{0:T(1024)}, u32[]{:S(2)}) copy-start(f32[1024]{0:T(1024)} %param.25) | copy-start | bytes 12292
  9.2 65.5 %copy-start.4 = (f32[1024]{0:T(1024)S(1)}, f32[1024]{0:T(1024)}, u32[]{:S(2)}) copy-start(f32[1024]{0:T(1024)} %param.24) | copy-start | bytes 12292
  9.2 444.3 %all-gather.6.cloned.1.call-start = ((), (), s32[]{:S(2)}) async-start(), calls=%async_computation.1 | async-start | bytes 50331648 | tf_op jit(solution)/shard_map/all_gather | solution.py:28
  9.9 530.3 %all-gather.8.cloned.1.call-start = ((), (), s32[]{:S(2)}) async-start(), calls=%async_computation.2 | async-start | bytes 4456448 | tf_op jit(solution)/shard_map/all_gather | solution.py:39
  75.0 395.8 %copy-start.7 = (f32[1024]{0:T(1024)S(1)}, f32[1024]{0:T(1024)}, u32[]{:S(2)}) copy-start(f32[1024]{0:T(1024)} %param.27) | copy-start | bytes 12292
  75.0 395.8 %copy-start.8 = (f32[1024]{0:T(1024)S(1)}, f32[1024]{0:T(1024)}, u32[]{:S(2)}) copy-start(f32[1024]{0:T(1024)} %param.26) | copy-start | bytes 12292
Sparse Core Ops, SparseCore 0:
  10.8 54.0 all-gather.3
  66.4 387.0 all-gather.5
  476.3 51.0 all-gather.7
where the time goes:
time: 568 us
  waiting for transfers between devices  379 us (67%)
  blocking collectives  126 us (22%)
  matrix products  45.2 us (8%)
  between operations  13.9 us (2%)
    all_gather x1, waiting for transfers between devices, body(): panel = lax.all_gather(base_weight, 'pop', axis=1, tiled=True)  379 us
    psum x2, blocking collectives, body(): proj = lax.psum(partial_value, 'blk').astype(jnp.bfloat16)  126 us
    dot_general x2, matrix products, body(): lax.dot_general(lax.all_gather(spike_rows, 'blk', axis=1, tiled=True), pa...  33.8 us
  transfers between devices with their start and end apart: 3, of which 1 were waited for; matrix products, arithmetic and copies ran while one was open for 1% of the time, Pallas kernels for 0%

commit v1 on v0

v1 whole, which is shorter than its diff:
```python
import functools

import jax
import jax.numpy as jnp
from jax import lax
from jax.experimental import pallas as pl
from jax.experimental.pallas import tpu as pltpu
from jax.sharding import PartitionSpec as P

STEPS = 2
CORES = 2
MESH = pl.DeviceIdType.MESH


def factor_plane(blks):
    chips = blks // CORES
    ys = 1
    while (2 * ys) * (2 * ys) <= chips:
        ys *= 2
    return ys, chips // ys


def kernel(
    pops, blks, halves, tiles,
    z_ref, part_ref, w_hbm, out_ref, proj_ref,
    gath, wbuf, acc, sendp, recvp, pg,
    w_sem, recv_sem, x_sem, up_sem, down_sem, y_sem, c_sem, ps_sem, pr_sem, ss_sem, sr_sem,
):
    ys, zs_all = factor_plane(blks)
    per = blks // pops
    group = ys * CORES
    srcs = per // group
    rows, block = z_ref.shape
    part = rows // halves
    outs = out_ref.shape[1]
    wide = outs // tiles

    p = lax.axis_index("pop")
    b = lax.axis_index("blk")
    c = lax.rem(b, CORES)
    y = lax.rem(b // CORES, ys)
    z = b // group
    mine = b // per
    first = p * srcs

    def at(pp, bb):
        return {"pop": pp, "blk": bb}

    def slot(i, pp, h):
        start = pl.multiple_of(pp * rows + h * part, part)
        return gath.at[i, pl.ds(start, part)]

    def index(i, pp, h):
        return (i * pops + pp) * halves + h

    def remote(src, dst, s_sem, r_sem, pp, bb):
        return pltpu.make_async_remote_copy(
            src_ref=src, dst_ref=dst, send_sem=s_sem, recv_sem=r_sem,
            device_id=at(pp, bb), device_id_type=MESH,
        )

    waits = []

    def send_if(cond, desc):
        if cond is None:
            desc.start()
        else:
            pl.when(cond)(desc.start)
        waits.append((cond, desc))

    my_i = lax.rem(b, per)
    for h in range(halves):
        src = z_ref.at[pl.ds(h * part, part)]
        r = recv_sem.at[index(my_i, p, h)]
        send_if(mine != p, remote(src, slot(my_i, p, h), x_sem.at[h], r, mine, b))

        @pl.when(mine == p)
        def _():
            pltpu.make_async_copy(src, slot(my_i, p, h), r).start()

    for d in range(1, blks):
        other = lax.rem(b + d, blks)
        send_if(None, remote(part_ref, pg.at[b], ps_sem.at[d], pr_sem.at[b], p, other))

    def w_copy(i):
        cols = pl.ds(pl.multiple_of(i * block, block), block)
        return pltpu.make_async_copy(w_hbm.at[:, cols], wbuf.at[i], w_sem.at[i])

    flip = z > first

    def source_of(g):
        return jnp.where(flip, srcs - 1 - g, g)

    for g in range(srcs):
        for j in range(group):
            w_copy(source_of(g) * group + j).start()
    acc[...] = jnp.zeros_like(acc)

    def arrive(i, pp, h):
        ref = slot(i, pp, h)
        k = index(i, pp, h)
        remote(ref, ref, x_sem.at[0], recv_sem.at[k], p, lax.rem(b + 1, blks)).wait_recv()

    def pass_on(i, pp, h, sem, cond, bb):
        k = index(i, pp, h)
        ref = slot(i, pp, h)
        send_if(cond, remote(ref, ref, sem, recv_sem.at[k], p, bb))

    def sibling():
        return (z * ys + y) * CORES + (1 - c)

    def line(g, pp, h):
        zs = source_of(g)
        i = zs * group + y * CORES + c
        k = index(i, pp, h)
        arrive(i, pp, h)
        origin = first + zs
        pass_on(i, pp, h, up_sem.at[k], (z >= origin) & (z < zs_all - 1), b + group)
        pass_on(i, pp, h, down_sem.at[k], (z <= origin) & (z > 0), b - group)
        for d in range(1, ys):
            other = (z * ys + lax.rem(y + d, ys)) * CORES + c
            pass_on(i, pp, h, y_sem.at[d, k], None, other)
        pass_on(i, pp, h, c_sem.at[k], None, sibling())

    def across(g, pp, h):
        for d in range(1, ys):
            i = source_of(g) * group + lax.rem(y + d, ys) * CORES + c
            arrive(i, pp, h)
            pass_on(i, pp, h, c_sem.at[index(i, pp, h)], None, sibling())

    def tile_dot(i, t):
        cols = pl.ds(t * wide if isinstance(t, int) else pl.multiple_of(t * wide, wide), wide)
        acc[:, cols] += lax.dot_general(
            gath[i], wbuf[i, cols, :], (((1,), (1,)), ((), ())),
            preferred_element_type=jnp.float32,
        )

    def other_core(g, yy):
        i = source_of(g) * group + yy * CORES + (1 - c)
        for q in range(pops):
            for h in range(halves):
                arrive(i, q, h)

    def ready(g):
        jobs = []
        for d in range(ys):
            yy = lax.rem(y + d, ys)
            jobs.append((source_of(g) * group + yy * CORES + c, None))
            jobs.append((source_of(g) * group + yy * CORES + (1 - c), yy))
        return [(g, i, yy) for i, yy in jobs]

    def multiply(job):
        g, i, yy = job
        if yy is not None:
            other_core(g, yy)
        w_copy(i).wait()

        @pl.loop(0, tiles)
        def _(t):
            tile_dot(i, t)

    steps = [(g, e, h) for g in range(srcs) for e in range(pops) for h in range(halves)]
    queue = []
    last = None
    for n, (g, e, h) in enumerate(steps):
        line(g, lax.rem(p + e, pops), h)
        if last is not None:
            across(last[0], lax.rem(p + last[1], pops), last[2])
            if last[0] != g:
                queue.extend(ready(last[0]))
        last = (g, e, h)
        if queue:
            multiply(queue.pop(0))
    across(last[0], lax.rem(p + last[1], pops), last[2])
    for job in queue:
        multiply(job)

    final = ready(srcs - 1)
    for g, i, yy in final:
        if yy is not None:
            other_core(g, yy)
        w_copy(i).wait()
    for t in range(tiles):
        for g, i, yy in final:
            tile_dot(i, t)
        for d in range(1, pops):
            pp = lax.rem(p + d, pops)
            half = acc[pl.ds(pl.multiple_of(pp * rows, rows), rows), pl.ds(t * wide, wide)]
            sendp[t, d] = half.astype(sendp.dtype)
            send_if(None, remote(
                sendp.at[t, d], recvp.at[t, p], ss_sem.at[t, d], sr_sem.at[t, p], pp, b))

    pg[b] = part_ref[...]
    for d in range(1, blks):
        other = lax.rem(b + d, blks)
        remote(part_ref, pg.at[other], ps_sem.at[d], pr_sem.at[other], p, other).wait_recv()
    total = pg[0]
    for d in range(1, blks):
        total = total + pg[d]
    proj_ref[...] = total

    for t in range(tiles):
        cols = pl.ds(t * wide, wide)
        value = acc[pl.ds(pl.multiple_of(p * rows, rows), rows), cols]
        for d in range(1, pops):
            pp = lax.rem(p + d, pops)
            remote(
                sendp.at[t, d], recvp.at[t, pp], ss_sem.at[t, d], sr_sem.at[t, pp], pp, b
            ).wait_recv()
            value = value + recvp[t, pp].astype(jnp.float32)
        out_ref[:, cols] = value

    for cond, desc in waits:
        if cond is None:
            desc.wait_send()
        else:
            pl.when(cond)(desc.wait_send)


def exchange(pops, blks, spikes, part, weight):
    rows, block = spikes.shape
    outs = weight.shape[0]
    per = blks // pops
    ys, _ = factor_plane(blks)
    halves = 2
    tiles = max(1, outs // 256)
    slots = blks * halves
    dma = pltpu.SemaphoreType.DMA
    vmem = pl.BlockSpec(memory_space=pltpu.VMEM)
    flops = 2 * pops * rows * weight.size
    return pl.pallas_call(
        functools.partial(kernel, pops, blks, halves, tiles),
        out_shape=(
            jax.ShapeDtypeStruct((rows, outs), jnp.float32),
            jax.ShapeDtypeStruct(part.shape, jnp.float32),
        ),
        in_specs=[vmem, vmem, pl.BlockSpec(memory_space=pl.ANY)],
        out_specs=(vmem, vmem),
        scratch_shapes=[
            pltpu.VMEM((per, pops * rows, block), spikes.dtype),
            pltpu.VMEM((per, outs, block), weight.dtype),
            pltpu.VMEM((pops * rows, outs), jnp.float32),
            pltpu.VMEM((tiles, pops, rows, outs // tiles), jnp.bfloat16),
            pltpu.VMEM((tiles, pops, rows, outs // tiles), jnp.bfloat16),
            pltpu.VMEM((blks,) + part.shape, jnp.float32),
            dma((per,)),
            dma((slots,)),
            dma((halves,)),
            dma((slots,)),
            dma((slots,)),
            dma((ys, slots)),
            dma((slots,)),
            dma((blks,)),
            dma((blks,)),
            dma((tiles, pops)),
            dma((tiles, pops)),
        ],
        compiler_params=pltpu.CompilerParams(
            has_side_effects=True, vmem_limit_bytes=40 * 2**20
        ),
        cost_estimate=pl.CostEstimate(
            flops=flops, bytes_accessed=weight.size * 2, transcendentals=0
        ),
    )(spikes, part, weight)


def body(
    pops,
    blks,
    v_init,
    a_init,
    z_init,
    base_weight,
    factor_u,
    factor_v,
    in_weight,
    spikes_in,
    step_count,
    member_ids,
    decay_mem,
    decay_adapt,
    thr_base,
    thr_adapt,
):
    members, trials, block = v_init.shape
    rank = factor_v.shape[1]
    rows = members * trials
    sign = (1 - 2 * (member_ids % 2)).astype(jnp.float32)
    state_v, state_a, spikes = (v_init, a_init, z_init)
    pad = -members % 128
    for step in range(STEPS):
        spikes_f = spikes.astype(jnp.float32)
        part = jnp.einsum(
            "mtn,mkn->tkm", spikes, factor_v, preferred_element_type=jnp.float32
        ).reshape(trials * rank, members)
        part = jnp.pad(part, ((0, 0), (0, pad)))
        dense, total = exchange(pops, blks, spikes.reshape(rows, block), part, base_weight)
        dense = dense.reshape(members, trials, block)
        proj = total[:, :members].reshape(trials, rank, members).astype(jnp.bfloat16)
        low = jnp.einsum("tkm,mkn->mtn", proj, factor_u, preferred_element_type=jnp.float32)
        current = jnp.dot(
            spikes_in[step].astype(jnp.bfloat16), in_weight, preferred_element_type=jnp.float32
        )
        drive = dense + 0.5 * sign[:, None, None] * low + current[None]
        v_new = (
            decay_mem * state_v
            + (1.0 - decay_mem) * drive
            - spikes_f * (thr_base + thr_adapt * state_a)
        )
        a_new = decay_adapt * state_a + (1.0 - decay_adapt) * spikes_f
        active = (step_count > step)[:, :, None]
        state_v = jnp.where(active, v_new, state_v)
        state_a = jnp.where(active, a_new, state_a)
        if step + 1 < STEPS:
            spikes = jax.nn.sigmoid(3.0 * (state_v - thr_base - thr_adapt * state_a)).astype(
                jnp.bfloat16
            )
    return (state_v, state_a)


def solution(mesh):
    in_specs = (
        P("pop", None, "blk"),
        P("pop", None, "blk"),
        P("pop", None, "blk"),
        P("blk", "pop"),
        P("pop", None, "blk"),
        P("pop", None, "blk"),
        P(None, "blk"),
        P(),
        P("pop", None),
        P("pop"),
        P("blk"),
        P("blk"),
        P("blk"),
        P("blk"),
    )
    out_specs = (P("pop", None, "blk"), P("pop", None, "blk"))
    return jax.shard_map(
        functools.partial(body, mesh.shape["pop"], mesh.shape["blk"]),
        mesh=mesh, in_specs=in_specs, out_specs=out_specs, check_vma=False,
    )
```

time: 568 us -> 127 us (0.22)
  waiting for transfers between devices: 379 us -> 0 us
  blocking collectives: 126 us -> 0 us
  Pallas kernels: 0 us -> 109 us
  matrix products: 45.2 us -> 11.3 us
  between operations: 13.9 us -> 0.82 us
    all_gather x3 -> x0, waiting for transfers between devices: 379 us -> none  [the longest x1 379 us: body(): panel = lax.all_gather(base_weight, 'pop', axis=1, tiled=True)]
    psum x2 -> x0, blocking collectives: 126 us -> none  [body(): proj = lax.psum(partial_value, 'blk').astype(jnp.bfloat16)]
    pallas_call x0 -> x2, Pallas kernels: none -> 109 us  [exchange(): pl.pallas_call(functools.partial(kernel, pops, blks, halves, tiles), out_...]
    dot_general x6 -> x4, matrix products: 44.6 us -> 10.7 us  [the longest x2 8.36 us: body(): jnp.einsum('tkm,mkn->mtn', proj, factor_u, preferred_element_type=jnp.flo...]
  transfers between devices with their start and end apart: 3 -> 0, of which waited for: 1 -> 0; matrix products, arithmetic and copies ran while one was open for 1% -> 0% of each run, Pallas kernels for 0% -> 0%
where the time goes in v1:
time: 127 us; the launch traced here: 126 us
  Pallas kernels  109 us (86%)
  matrix products  11.3 us (9%)
  local copies, waits for them, and re-layouts  3.38 us (3%)
  other arithmetic  1.53 us (1%)
    pallas_call x2, Pallas kernels, exchange(): pl.pallas_call(functools.partial(kernel, pops, blks, halves, tiles), out_...  109 us
    dot_general x2, matrix products, body(): jnp.einsum('tkm,mkn->mtn', proj, factor_u, preferred_element_type=jnp.flo...  8.36 us

profile of v1, /device:TPU:0, one launch (start us, length us, event | category | flops | bytes accessed | tf_op | source)
XLA Modules:
  0.0 126.5 jit_solution(1617874013480679268)
XLA Ops:
  0.6 0.0 copy-start
  0.6 0.8 broadcast_compare_fusion.1
  1.4 0.1 copy.16
  1.6 0.1 copy.17
  1.7 0.7 broadcast_subtract_fusion
  2.4 1.0 reshape.40.z_ref
  3.4 1.7 %convolution_bitcast_fusion.1 = f32[2,4,64]{1,0,2:T(2,128)S(1)} fusion(bf16[64,4,1024]{2,1,0:T(4,128)(2,1)} %param.19, bf16[64,2,1024]{2,1,0:T(2,128)(2,1)} %param.16), kind=kOutput, calls=%fused_computation.11 | convolution fusion | flops 1048576 | bytes 788480 | tf_op jit(solution)/shard_map/mtn,mkn->tkm/dot_general | solution.py:293
  5.2 0.1 copy.18
  5.3 0.0 copy-start.2
  5.3 57.1 %shard_map.149 = (f32[128,1024]{1,0:T(8,128)S(1)}, f32[8,128]{1,0:T(8,128)S(1)}) custom-call(bf16[128,1024]{1,0:T(8,128)(2,1)S(1)} %reshape.40.z_ref, f32[8,128]{1,0:T(8,128)S(1)} %pad.7.part_ref, bf16[1024,8192]{1,0:T(8,128)(2,1)} %w_hbm.3), custom_call_target="tpu_custom_call" | custom-call | flops 4294967296 | bytes 16777216 | tf_op jit(solution)/shard_map/pallas_call | solution.py:231
  62.4 0.0 copy-start.10
  62.4 0.0 copy-start.1
  62.4 0.0 copy-start.3
  62.4 0.0 copy-start.4
  62.4 0.0 copy-start.8
  62.5 0.0 copy-start.9
  62.5 0.3 reshape.42
  62.8 0.1 copy.19
  62.9 0.0 copy-done.2
  62.9 0.0 copy-done
  63.0 0.3 fusion.18
  63.3 0.0 copy-done.10
  63.3 0.1 copy-done.1
  63.4 0.0 copy-done.3
  63.4 0.0 copy-done.4
  63.4 0.0 copy-done.8
  63.4 0.0 copy-done.9
  63.4 0.0 copy-start.5
  63.4 4.7 %fusion.15 = (f32[64,2,1024]{2,1,0:T(2,128)}, bf16[64,2,1024]{2,1,0:T(2,128)(2,1)S(1)}, f32[64,2,1024]{2,1,0:T(2,128)}) fusion(pred[64,2]{1,0:T(8,128)(4,1)S(1)} %copy.16, f32[1024]{0:T(1024)S(1)} %get-tuple-element.15, f32[1024]{0:T(1024)S(1)} %copy-done.3, f32[64,2,1024]{2,1,0:T(2,128)} %param.15, bf16[64,2,1024]{2,1,0:T(2,128)(2,1)S(1)} %copy-done.1, ...), kind=kOutput, calls=%fused_computation.23 | convolution fusion | flops 4849664 | bytes 3704320 | tf_op jit(solution)/shard_map/tkm,mkn->mtn/dot_general | solution.py:300
  68.1 0.1 reshape.43.z_ref
  68.2 0.0 copy-done.5
  68.2 0.6 convolution_bitcast_fusion
  68.8 0.1 copy.20
  68.9 52.3 %shard_map.150 = (f32[128,1024]{1,0:T(8,128)S(1)}, f32[8,128]{1,0:T(8,128)S(1)}) custom-call(bf16[128,1024]{1,0:T(8,128)(2,1)S(1)} %reshape.43.z_ref, f32[8,128]{1,0:T(8,128)S(1)} %pad.8.part_ref, bf16[1024,8192]{1,0:T(8,128)(2,1)} %w_hbm.3), custom_call_target="tpu_custom_call" | custom-call | flops 4294967296 | bytes 16777216 | tf_op jit(solution)/shard_map/pallas_call | solution.py:231
  121.3 0.3 reshape.45
  121.6 0.0 copy-start.6
  121.6 0.1 copy.21
  121.7 0.0 copy-start.7
  121.8 0.3 fusion.17
  122.1 0.6 copy-done.6
  122.6 0.2 copy-done.7
  122.8 3.6 %fusion.11 = f32[64,2,1024]{2,1,0:T(2,128)} fusion(f32[64,2,1024]{2,1,0:T(2,128)} %get-tuple-element.14, f32[64,2,1024]{2,1,0:T(2,128)S(1)} %reshape.45, bf16[2,4,64]{1,0,2:T(2,128)(2,1)S(1)} %copy.21, bf16[64,4,1024]{2,1,0:T(4,128)(2,1)S(1)} %copy-done.7, bf16[64,2,1024]{2,1,0:T(2,128)(2,1)S(1)} %get-tuple-element.11, pred[64,2]{1,0:T(8,128)(4,1)S(1)} %copy.16, ...), kind=kOutput, calls=%fused_computation.15 | convolution fusion | flops 3276800 | bytes 3180032 | tf_op jit(solution)/shard_map/tkm,mkn->mtn/dot_general | solution.py:300
  (6 shorter events, 0.0 us)
Async XLA Ops:
  0.6 62.3 %copy-start = (bf16[700,1024]{1,0:T(8,128)(2,1)S(1)}, bf16[700,1024]{1,0:T(8,128)(2,1)}, u32[]{:S(2)}) copy-start(bf16[700,1024]{1,0:T(8,128)(2,1)} %param.20) | copy-start | bytes 4300804
  5.3 57.7 %copy-start.2 = (s32[2,2,700]{2,1,0:T(2,128)S(1)}, s32[2,2,700]{2,1,0:T(2,128)}, u32[]{:S(2)}) copy-start(s32[2,2,700]{2,1,0:T(2,128)} %param.21) | copy-start | bytes 33604
  62.4 0.9 copy-start.10
  62.4 1.0 copy-start.1
  62.4 0.9 copy-start.3
  62.4 0.9 copy-start.4
  62.4 0.9 copy-start.8
  62.5 0.9 copy-start.9
  63.4 4.8 %copy-start.5 = (bf16[64,4,1024]{2,1,0:T(4,128)(2,1)S(1)}, bf16[64,4,1024]{2,1,0:T(4,128)(2,1)}, u32[]{:S(2)}) copy-start(bf16[64,4,1024]{2,1,0:T(4,128)(2,1)} %param.19) | copy-start | bytes 1572868
  121.6 1.0 copy-start.6
  121.7 1.1 copy-start.7

commit v2 on v1

--- a/solution.py
+++ b/solution.py
@@ -286,36 +286,37 @@
     rank = factor_v.shape[1]
     rows = members * trials
     sign = (1 - 2 * (member_ids % 2)).astype(jnp.float32)
-    state_v, state_a, spikes = (v_init, a_init, z_init)
+    turn = lambda x: x.transpose(1, 0, 2)
+    state_v, state_a, spikes = (turn(v_init), turn(a_init), turn(z_init))
     pad = -members % 128
     for step in range(STEPS):
         spikes_f = spikes.astype(jnp.float32)
         part = jnp.einsum(
-            "mtn,mkn->tkm", spikes, factor_v, preferred_element_type=jnp.float32
+            "tmn,mkn->tkm", spikes, factor_v, preferred_element_type=jnp.float32
         ).reshape(trials * rank, members)
         part = jnp.pad(part, ((0, 0), (0, pad)))
         dense, total = exchange(pops, blks, spikes.reshape(rows, block), part, base_weight)
-        dense = dense.reshape(members, trials, block)
+        dense = dense.reshape(trials, members, block)
         proj = total[:, :members].reshape(trials, rank, members).astype(jnp.bfloat16)
-        low = jnp.einsum("tkm,mkn->mtn", proj, factor_u, preferred_element_type=jnp.float32)
+        low = jnp.einsum("tkm,mkn->tmn", proj, factor_u, preferred_element_type=jnp.float32)
         current = jnp.dot(
             spikes_in[step].astype(jnp.bfloat16), in_weight, preferred_element_type=jnp.float32
         )
-        drive = dense + 0.5 * sign[:, None, None] * low + current[None]
+        drive = dense + 0.5 * sign[None, :, None] * low + current[:, None]
         v_new = (
             decay_mem * state_v
             + (1.0 - decay_mem) * drive
             - spikes_f * (thr_base + thr_adapt * state_a)
         )
         a_new = decay_adapt * state_a + (1.0 - decay_adapt) * spikes_f
-        active = (step_count > step)[:, :, None]
+        active = (step_count > step).T[:, :, None]
         state_v = jnp.where(active, v_new, state_v)
         state_a = jnp.where(active, a_new, state_a)
         if step + 1 < STEPS:
             spikes = jax.nn.sigmoid(3.0 * (state_v - thr_base - thr_adapt * state_a)).astype(
                 jnp.bfloat16
             )
-    return (state_v, state_a)
+    return (turn(state_v), turn(state_a))
 
 
 def solution(mesh):

time: 127 us -> 129 us (1.016)
  other arithmetic: 1.53 us -> 4.41 us
    transpose x0 -> x2, other arithmetic: none -> 3.1 us  [the longest x1 2.31 us: body(): turn = lambda x: x.transpose(1, 0, 2)]
    dot_general x4, matrix products: 10.7 us -> 8.83 us  [the longest x2 5.44 us: body(): jnp.einsum('tkm,mkn->tmn', proj, factor_u, preferred_element_type=jnp.flo...]
    reshape x4 -> x0, local copies, waits for them, and re-layouts: 1.76 us -> none  [the longest x2 1.15 us: body(): spikes.reshape(rows, block)]
where the time goes in v2:
time: 129 us
  Pallas kernels  109 us (84%)
  matrix products  10.2 us (8%)
  other arithmetic  4.41 us (3%)
  local copies, waits for them, and re-layouts  3.75 us (3%)
    pallas_call x2, Pallas kernels, exchange(): pl.pallas_call(functools.partial(kernel, pops, blks, halves, tiles), out_...  109 us
    dot_general x2, matrix products, body(): jnp.einsum('tkm,mkn->tmn', proj, factor_u, preferred_element_type=jnp.flo...  5.44 us
    dot_general x2, matrix products, body(): jnp.einsum('tmn,mkn->tkm', spikes, factor_v, preferred_element_type=jnp.f...  3.39 us

profile of v2, /device:TPU:0, one launch (start us, length us, event | category | flops | bytes accessed | tf_op | source)
XLA Modules:
  0.0 128.7 jit_solution(4403558806356672523)
XLA Ops:
  0.6 0.0 copy-start
  0.6 0.8 compare_bitcast_fusion.1
  1.4 0.1 copy.17
  1.6 0.7 broadcast_subtract_fusion
  2.3 1.0 copy.18
  3.3 1.7 %convolution_bitcast_fusion.1 = f32[2,4,64]{1,0,2:T(2,128)S(1)} fusion(bf16[64,4,1024]{2,1,0:T(4,128)(2,1)} %param.19, bf16[64,2,1024]{2,1,0:T(2,128)(2,1)} %param.16), kind=kOutput, calls=%fused_computation.13 | convolution fusion | flops 1048576 | bytes 788480 | tf_op jit(solution)/shard_map/tmn,mkn->tkm/dot_general | solution.py:294
  5.0 0.1 copy.19
  5.1 57.1 %shard_map.149 = (f32[128,1024]{1,0:T(8,128)S(1)}, f32[8,128]{1,0:T(8,128)S(1)}) custom-call(bf16[128,1024]{1,0:T(8,128)(2,1)S(1)} %bitcast.102, f32[8,128]{1,0:T(8,128)S(1)} %pad.7.part_ref, bf16[1024,8192]{1,0:T(8,128)(2,1)} %w_hbm.3), custom_call_target="tpu_custom_call" | custom-call | flops 4294967296 | bytes 16777216 | tf_op jit(solution)/shard_map/pallas_call | solution.py:231
  62.3 0.0 copy-start.21
  62.3 0.0 copy-start.1
  62.3 0.0 copy-start.2
  62.3 0.0 copy-start.12
  62.3 0.0 copy-start.14
  62.3 0.0 copy-start.16
  62.3 0.1 copy.20
  62.5 0.0 copy-done.11
  62.5 0.0 copy-done
  62.5 0.0 copy-start.6
  62.5 0.3 fusion.23
  62.8 0.3 copy-done.6
  63.1 0.0 copy-done.21
  63.1 0.0 copy-done.18
  63.1 0.1 copy-done.1
  63.2 0.2 copy-done.2
  63.5 0.0 copy-done.12
  63.5 0.0 copy-done.14
  63.5 0.0 copy-done.16
  63.5 0.0 copy-start.7
  63.5 2.8 %fusion.12 = f32[2,64,1024]{2,0,1:T(2,128)S(1)} fusion(bf16[2,4,64]{1,0,2:T(2,128)(2,1)S(1)} %copy.20, bf16[64,4,1024]{2,1,0:T(4,128)(2,1)} %param.18, f32[64,2,1024]{2,1,0:T(2,128)S(1)} %copy-done.2, f32[64,2,1024]{2,1,0:T(2,128)} %param.14, f32[2,64,1024]{2,1,0:T(8,128)S(1)} %bitcast.104, pred[2,64]{0,1:T(8,128)(4,1)S(1)} %copy.17, f32[64]{0:T(128)S(1)} %fusion.27, ...), kind=kOutput, calls=%fused_computation.16 | convolution fusion | flops 2621440 | bytes 2909568 | tf_op jit(solution)/shard_map/tkm,mkn->tmn/dot_general | solution.py:301
  66.3 0.0 copy-done.22
  66.3 0.0 copy-start.3
  66.3 0.1 copy.16
  66.4 0.0 copy-done.9
  66.4 2.3 %fusion.19 = (f32[64,2,1024]{2,1,0:T(2,128)}, bf16[2,64,1024]{2,0,1:T(2,128)(2,1)S(1)}) fusion(pred[2,64]{0,1:T(8,128)(4,1)S(1)} %copy.16, f32[1024]{0:T(1024)S(1)} %get-tuple-element.14, f32[1024]{0:T(1024)S(1)} %copy-done.7, bf16[64,2,1024]{2,1,0:T(2,128)(2,1)S(1)} %copy-done.1, f32[64,2,1024]{2,1,0:T(2,128)S(1)} %copy-done.2, pred[2,64]{0,1:T(8,128)(4,1)S(1)} %copy.17, ...), kind=kLoop, calls=%fused_computation.27 | loop fusion | flops 2359296 | bytes 2113792 | tf_op jit(solution)/shard_map/transpose | solution.py:289
  68.7 0.0 copy-done.3
  68.8 1.7 %convolution_bitcast_fusion = f32[2,4,64]{1,0,2:T(2,128)S(1)} fusion(bf16[2,64,1024]{2,0,1:T(2,128)(2,1)S(1)} %get-tuple-element.11, bf16[64,4,1024]{2,1,0:T(4,128)(2,1)} %param.19), kind=kOutput, calls=%fused_computation.12 | convolution fusion | flops 1048576 | bytes 788480 | tf_op jit(solution)/shard_map/tmn,mkn->tkm/dot_general | solution.py:294
  70.5 0.1 copy.23
  70.6 52.4 %shard_map.150 = (f32[128,1024]{1,0:T(8,128)S(1)}, f32[8,128]{1,0:T(8,128)S(1)}) custom-call(bf16[128,1024]{1,0:T(8,128)(2,1)S(1)} %bitcast.101, f32[8,128]{1,0:T(8,128)S(1)} %pad.8.part_ref, bf16[1024,8192]{1,0:T(8,128)(2,1)} %w_hbm.3), custom_call_target="tpu_custom_call" | custom-call | flops 4294967296 | bytes 16777216 | tf_op jit(solution)/shard_map/pallas_call | solution.py:231
  122.9 0.0 copy-start.4
  122.9 0.6 convert.12
  123.5 1.4 %copy.24 = bf16[2,4,64]{1,0,2:T(2,128)(2,1)} copy(bf16[2,4,64]{2,1,0:T(4,128)(2,1)} %bitcast.109) | data formatting | bytes 2048 | tf_op jit(solution)/shard_map/convert_element_type | solution.py:300
  124.9 0.0 copy-start.15
  124.9 0.0 copy-start.17
  125.0 0.0 copy-start.20
  125.0 0.0 copy-start.23
  125.0 1.0 fusion.22
  126.0 0.0 copy-done.4
  126.1 2.6 %fusion.14 = f32[64,2,1024]{2,1,0:T(2,128)} fusion(f32[2,64,1024]{2,0,1:T(2,128)S(1)} %copy-done.4, bf16[2,4,64]{1,0,2:T(2,128)(2,1)S(1)} %copy-done.5, bf16[64,4,1024]{2,1,0:T(4,128)(2,1)S(1)} %copy-done.20, bf16[2,64,1024]{2,0,1:T(2,128)(2,1)S(1)} %get-tuple-element.11, f32[2,64,1024]{2,1,0:T(8,128)S(1)} %bitcast.103, pred[2,64]{0,1:T(8,128)(4,1)S(1)} %copy.16, ...), kind=kOutput, calls=%fused_computation.18 | convolution fusion | flops 3276800 | bytes 3180032 | tf_op jit(solution)/shard_map/tkm,mkn->tmn/dot_general | solution.py:301
  (25 shorter events, 0.1 us)
Async XLA Ops:
  0.6 61.9 %copy-start = (bf16[700,1024]{1,0:T(8,128)(2,1)S(1)}, bf16[700,1024]{1,0:T(8,128)(2,1)}, u32[]{:S(2)}) copy-start(bf16[700,1024]{1,0:T(8,128)(2,1)} %param.20) | copy-start | bytes 4300804
  2.3 60.8 %copy-start.18 = (f32[1024]{0:T(1024)}, f32[1024]{0:T(1024)S(1)}, u32[]{:S(2)}) copy-start(f32[1024]{0:T(1024)S(1)} %get-tuple-element.15) | copy-start | bytes 12292
  2.3 64.2 %copy-start.9 = (f32[1024]{0:T(1024)}, f32[1024]{0:T(1024)S(1)}, u32[]{:S(2)}) copy-start(f32[1024]{0:T(1024)S(1)} %get-tuple-element.14) | copy-start | bytes 12292
  5.1 57.4 %copy-start.11 = (s32[2,2,700]{2,1,0:T(2,128)S(1)}, s32[2,2,700]{2,1,0:T(2,128)}, u32[]{:S(2)}) copy-start(s32[2,2,700]{2,1,0:T(2,128)} %param.21) | copy-start | bytes 33604
  62.3 0.8 copy-start.21
  62.3 1.0 copy-start.1
  62.3 1.2 copy-start.2
  62.3 1.2 copy-start.12
  62.3 1.2 copy-start.14
  62.3 1.2 copy-start.16
  62.5 0.6 copy-start.6
  63.5 2.8 %copy-start.22 = (f32[64]{0:T(128)}, f32[64]{0:T(128)S(1)}, u32[]{:S(2)}) copy-start(f32[64]{0:T(128)S(1)} %fusion.27) | copy-start | bytes 772
  63.5 3.0 %copy-start.7 = (f32[1024]{0:T(1024)S(1)}, f32[1024]{0:T(1024)}, u32[]{:S(2)}) copy-start(f32[1024]{0:T(1024)} %param.25) | copy-start | bytes 12292
  66.3 2.5 %copy-start.3 = (f32[2,64,1024]{2,0,1:T(2,128)}, f32[2,64,1024]{2,0,1:T(2,128)S(1)}, u32[]{:S(2)}) copy-start(f32[2,64,1024]{2,0,1:T(2,128)S(1)} %fusion.12) | copy-start | bytes 1572868
  122.9 3.1 %copy-start.4 = (f32[2,64,1024]{2,0,1:T(2,128)S(1)}, f32[2,64,1024]{2,0,1:T(2,128)}, u32[]{:S(2)}) copy-start(f32[2,64,1024]{2,0,1:T(2,128)} %copy-done.3) | copy-start | bytes 1572868
  124.9 1.1 copy-start.5
  124.9 1.1 copy-start.8
  124.9 1.1 copy-start.10
  124.9 1.1 copy-start.13
  124.9 1.1 copy-start.15
  124.9 1.1 copy-start.17
  124.9 1.1 copy-start.19
  125.0 1.1 copy-start.20
  125.0 1.1 copy-start.23

commit v3 on v1

--- a/solution.py
+++ b/solution.py
@@ -171,11 +171,13 @@
         last = (g, e, h)
         if queue:
             multiply(queue.pop(0))
-    across(last[0], lax.rem(p + last[1], pops), last[2])
     for job in queue:
         multiply(job)
-
     final = ready(srcs - 1)
+    multiply(final[0])
+    across(last[0], lax.rem(p + last[1], pops), last[2])
+    multiply(final[1])
+    final = final[2:]
     for g, i, yy in final:
         if yy is not None:
             other_core(g, yy)

time: 127 us -> 129 us (1.016)
  Pallas kernels: 109 us -> 112 us
    pallas_call x2, Pallas kernels: 109 us -> 112 us  [exchange(): pl.pallas_call(functools.partial(kernel, pops, blks, halves, tiles), out_...]
where the time goes in v3:
time: 129 us
  Pallas kernels  112 us (87%)
  matrix products  11.3 us (9%)
  local copies, waits for them, and re-layouts  3.38 us (3%)
  other arithmetic  1.53 us (1%)
    pallas_call x2, Pallas kernels, exchange(): pl.pallas_call(functools.partial(kernel, pops, blks, halves, tiles), out_...  112 us
    dot_general x2, matrix products, body(): jnp.einsum('tkm,mkn->mtn', proj, factor_u, preferred_element_type=jnp.flo...  8.36 us

profile of v3, /device:TPU:0, one launch (start us, length us, event | category | flops | bytes accessed | tf_op | source)
XLA Modules:
  0.0 128.6 jit_solution(13474203182848897627)
XLA Ops:
  0.6 0.0 copy-start
  0.6 0.8 broadcast_compare_fusion.1
  1.4 0.1 copy.16
  1.6 0.1 copy.17
  1.7 0.7 broadcast_subtract_fusion
  2.4 1.0 reshape.40.z_ref
  3.4 1.7 %convolution_bitcast_fusion.1 = f32[2,4,64]{1,0,2:T(2,128)S(1)} fusion(bf16[64,4,1024]{2,1,0:T(4,128)(2,1)} %param.19, bf16[64,2,1024]{2,1,0:T(2,128)(2,1)} %param.16), kind=kOutput, calls=%fused_computation.11 | convolution fusion | flops 1048576 | bytes 788480 | tf_op jit(solution)/shard_map/mtn,mkn->tkm/dot_general | solution.py:295
  5.2 0.1 copy.18
  5.3 0.0 copy-start.2
  5.3 58.2 %shard_map.149 = (f32[128,1024]{1,0:T(8,128)S(1)}, f32[8,128]{1,0:T(8,128)S(1)}) custom-call(bf16[128,1024]{1,0:T(8,128)(2,1)S(1)} %reshape.40.z_ref, f32[8,128]{1,0:T(8,128)S(1)} %pad.7.part_ref, bf16[1024,8192]{1,0:T(8,128)(2,1)} %w_hbm.3), custom_call_target="tpu_custom_call" | custom-call | flops 4294967296 | bytes 16777216 | tf_op jit(solution)/shard_map/pallas_call | solution.py:233
  63.4 0.0 copy-start.10
  63.4 0.0 copy-start.1
  63.5 0.0 copy-start.3
  63.5 0.0 copy-start.4
  63.5 0.0 copy-start.8
  63.5 0.0 copy-start.9
  63.5 0.3 reshape.42
  63.8 0.1 copy.19
  64.0 0.0 copy-done.2
  64.0 0.0 copy-done
  64.0 0.3 fusion.18
  64.3 0.0 copy-done.10
  64.3 0.1 copy-done.1
  64.4 0.0 copy-done.3
  64.4 0.0 copy-done.4
  64.4 0.0 copy-done.8
  64.4 0.0 copy-done.9
  64.4 0.0 copy-start.5
  64.4 4.7 %fusion.15 = (f32[64,2,1024]{2,1,0:T(2,128)}, bf16[64,2,1024]{2,1,0:T(2,128)(2,1)S(1)}, f32[64,2,1024]{2,1,0:T(2,128)}) fusion(pred[64,2]{1,0:T(8,128)(4,1)S(1)} %copy.16, f32[1024]{0:T(1024)S(1)} %get-tuple-element.15, f32[1024]{0:T(1024)S(1)} %copy-done.3, f32[64,2,1024]{2,1,0:T(2,128)} %param.15, bf16[64,2,1024]{2,1,0:T(2,128)(2,1)S(1)} %copy-done.1, ...), kind=kOutput, calls=%fused_computation.23 | convolution fusion | flops 4849664 | bytes 3704320 | tf_op jit(solution)/shard_map/tkm,mkn->mtn/dot_general | solution.py:302
  69.1 0.1 reshape.43.z_ref
  69.2 0.0 copy-done.5
  69.3 0.6 convolution_bitcast_fusion
  69.9 0.1 copy.20
  70.0 53.4 %shard_map.150 = (f32[128,1024]{1,0:T(8,128)S(1)}, f32[8,128]{1,0:T(8,128)S(1)}) custom-call(bf16[128,1024]{1,0:T(8,128)(2,1)S(1)} %reshape.43.z_ref, f32[8,128]{1,0:T(8,128)S(1)} %pad.8.part_ref, bf16[1024,8192]{1,0:T(8,128)(2,1)} %w_hbm.3), custom_call_target="tpu_custom_call" | custom-call | flops 4294967296 | bytes 16777216 | tf_op jit(solution)/shard_map/pallas_call | solution.py:233
  123.4 0.3 reshape.45
  123.7 0.0 copy-start.6
  123.8 0.1 copy.21
  123.9 0.0 copy-start.7
  123.9 0.3 fusion.17
  124.2 0.6 copy-done.6
  124.8 0.2 copy-done.7
  125.0 3.6 %fusion.11 = f32[64,2,1024]{2,1,0:T(2,128)} fusion(f32[64,2,1024]{2,1,0:T(2,128)} %get-tuple-element.14, f32[64,2,1024]{2,1,0:T(2,128)S(1)} %reshape.45, bf16[2,4,64]{1,0,2:T(2,128)(2,1)S(1)} %copy.21, bf16[64,4,1024]{2,1,0:T(4,128)(2,1)S(1)} %copy-done.7, bf16[64,2,1024]{2,1,0:T(2,128)(2,1)S(1)} %get-tuple-element.11, pred[64,2]{1,0:T(8,128)(4,1)S(1)} %copy.16, ...), kind=kOutput, calls=%fused_computation.15 | convolution fusion | flops 3276800 | bytes 3180032 | tf_op jit(solution)/shard_map/tkm,mkn->mtn/dot_general | solution.py:302
  (6 shorter events, 0.0 us)
Async XLA Ops:
  0.6 63.3 %copy-start = (bf16[700,1024]{1,0:T(8,128)(2,1)S(1)}, bf16[700,1024]{1,0:T(8,128)(2,1)}, u32[]{:S(2)}) copy-start(bf16[700,1024]{1,0:T(8,128)(2,1)} %param.20) | copy-start | bytes 4300804
  5.3 58.7 %copy-start.2 = (s32[2,2,700]{2,1,0:T(2,128)S(1)}, s32[2,2,700]{2,1,0:T(2,128)}, u32[]{:S(2)}) copy-start(s32[2,2,700]{2,1,0:T(2,128)} %param.21) | copy-start | bytes 33604
  63.4 0.9 copy-start.10
  63.4 1.0 copy-start.1
  63.5 0.9 copy-start.3
  63.5 0.9 copy-start.4
  63.5 0.9 copy-start.8
  63.5 0.9 copy-start.9
  64.4 4.8 %copy-start.5 = (bf16[64,4,1024]{2,1,0:T(4,128)(2,1)S(1)}, bf16[64,4,1024]{2,1,0:T(4,128)(2,1)}, u32[]{:S(2)}) copy-start(bf16[64,4,1024]{2,1,0:T(4,128)(2,1)} %param.19) | copy-start | bytes 1572868
  123.7 1.0 copy-start.6
  123.9 1.1 copy-start.7
